TPU v7x, 32 devices: a whole 2x2x4 slice. The times are simulated.
32 devices in a mesh: row: 4 (over x, core), col: 8 (over z, y).
Axes of the slice: x: 2, y: 2, z: 4, core: 2. Of those that a mesh axis runs over, the one named last changes fastest.
Arguments:
- local_load: float32 [4, 8, 1024, 256], P('row', 'col'), may hold values from -6 to 6
- schur_operator: float32 [4, 8, 1024, 1024], P('row', 'col'), may hold values from -1 to 5
- local_solver: float32 [4, 8, 1024, 1024], P('row', 'col'), may hold values from -1 to 1
- coarse_modes: float32 [4, 8, 32, 1024], P('row', 'col'), may hold values from -0.1875 to 0.1875
- coarse_inverse: float32 [4, 8, 4, 32, 256], P('row', 'col'), may hold values from -1 to 2
- share_rows: int32 [4, 8, 3, 3, 128], P('row', 'col'), may hold values from 0 to 1023, as said below
- share_count: int32 [4, 8, 3, 3], P('row', 'col'), may hold values from 0 to 128, as said below
- multiplicity: int32 [4, 8, 1024], P('row', 'col'), may hold values from 1 to 2, as said below
Outputs:
- iterate: float32 [4, 8, 1024, 256], P('row', 'col')
- residual: float32 [4, 8, 1024, 256], P('row', 'col')
Inputs may be any that keep to these rules, and one draw needn't show every extreme that they name: `share_rows`: within one subdomain no row lies in two lists, and only the first share_count entries of a list are meaningful. Entry m of the list of (a, b) toward (a + p - 1, b + q - 1) and entry m of that neighbour's list toward (a, b) name the same interface unknown. share_count[a, b, p, q] equals the neighbour's count toward (a, b); it is 0 for the centre and where no neighbour exists, at most 128 along a grid axis and at most 16 for a diagonal neighbour, and both bounds are reached. multiplicity is 2 on rows that lie in some list and 1 elsewhere.
All inputs are finite; a program needn't handle non-finite values.
Results may differ from a plain program's by a relative error of at most 0.0003.
Values sent between devices are 32-bit elements; how exact they have to be, the bound alone decides.
A program may use at most 128 MiB of HBM per device.

v0:
```python
import jax
import jax.numpy as jnp
from jax import lax
from jax.sharding import PartitionSpec as P

CORNER = 16
STEPS = 2


PRECISE = lax.Precision.HIGHEST


def passed_along(value, axis, steps):
    count = lax.axis_size(axis)
    leading, last = (max(0, -steps), min(count, count - steps))
    return lax.ppermute(value, axis, [(source, source + steps) for source in range(leading, last)])


def pad_rows(packet_rows, share_len):
    return jnp.pad(packet_rows, ((0, share_len - packet_rows.shape[0]), (0, 0)))


def neighbour_sum(values, rows_local, counts_local):
    share_len = rows_local.shape[-1]
    slot_ids = lax.broadcasted_iota(jnp.int32, rows_local.shape, 2)
    live_mask = (slot_ids < counts_local[..., None]).astype(jnp.float32)
    packets = values[rows_local] * live_mask[..., None]
    incoming = {}
    sideways = {}
    for heading in (1, -1):
        col_slot = 1 + heading
        bundle = jnp.concatenate(
            [packets[0, col_slot, :CORNER], packets[1, col_slot], packets[2, col_slot, :CORNER]],
            axis=0,
        )
        arrived = passed_along(bundle, "col", heading)
        sideways[heading] = arrived
        incoming[1, 1 - heading] = arrived[CORNER : CORNER + share_len]
    for heading in (1, -1):
        row_slot = 1 + heading
        offset = 0 if heading == -1 else CORNER + share_len
        from_left = sideways[1][offset : offset + CORNER]
        from_right = sideways[-1][offset : offset + CORNER]
        bundle = jnp.concatenate([from_left, packets[row_slot, 1], from_right], axis=0)
        arrived = passed_along(bundle, "row", heading)
        incoming[1 - heading, 0] = pad_rows(arrived[:CORNER], share_len)
        incoming[1 - heading, 1] = arrived[CORNER : CORNER + share_len]
        incoming[1 - heading, 2] = pad_rows(arrived[CORNER + share_len :], share_len)
    empty_rows = jnp.zeros((share_len, values.shape[1]), jnp.float32)
    ordered = [
        incoming.get((row_slot, col_slot), empty_rows)
        for row_slot in range(3)
        for col_slot in range(3)
    ]
    stacked = jnp.concatenate(ordered, axis=0)
    return values.at[rows_local.reshape(-1)].add(stacked)


def coarse_solve(coarse_rhs, tile_rows):
    own_count = coarse_rhs.shape[0]
    partial_sol = lax.dot_general(
        tile_rows,
        lax.all_gather(coarse_rhs, "row", axis=0, tiled=True),
        (((0,), (0,)), ((), ())),
        precision=PRECISE,
        preferred_element_type=jnp.float32,
    )
    summed = lax.psum(partial_sol, "col")
    column = lax.axis_index("col")
    return lax.dynamic_slice_in_dim(summed, column * own_count, own_count, 0)


def on_device(
    local_load,
    schur_operator,
    local_solver,
    coarse_modes,
    coarse_inverse,
    share_rows,
    share_count,
    multiplicity,
):
    rows_local = share_rows[0, 0]
    counts_local = share_count[0, 0]
    matrix_schur = schur_operator[0, 0]
    matrix_solver = local_solver[0, 0]
    modes_local = coarse_modes[0, 0]
    coarse_tile = coarse_inverse[0, 0]
    tile_rows = coarse_tile.reshape(-1, coarse_tile.shape[-1])
    weight = (1.0 / multiplicity[0, 0].astype(jnp.float32))[:, None]

    def assemble(values):
        return neighbour_sum(values, rows_local, counts_local)

    def apply_matrix(matrix, values):
        return jnp.dot(matrix, values, precision=PRECISE, preferred_element_type=jnp.float32)

    residual = assemble(local_load[0, 0])
    iterate = jnp.zeros_like(residual)
    for step_index in range(STEPS):
        coarse_rhs = apply_matrix(modes_local, weight * residual)
        coarse_sol = coarse_solve(coarse_rhs, tile_rows)
        spread_values = weight * lax.dot_general(
            modes_local,
            coarse_sol,
            (((0,), (0,)), ((), ())),
            precision=PRECISE,
            preferred_element_type=jnp.float32,
        )
        correction = assemble(spread_values)
        iterate = iterate + correction
        residual = residual - assemble(apply_matrix(matrix_schur, correction))
        update = assemble(weight * apply_matrix(matrix_solver, weight * residual))
        iterate = iterate + update
        residual = residual - assemble(apply_matrix(matrix_schur, update))
    return (iterate[None, None], residual[None, None])


def solution(mesh):
    in_specs = (
        P("row", "col", None, None),
        P("row", "col", None, None),
        P("row", "col", None, None),
        P("row", "col", None, None),
        P("row", "col", None, None, None),
        P("row", "col", None, None, None),
        P("row", "col", None, None),
        P("row", "col", None),
    )
    out_specs = (P("row", "col", None, None), P("row", "col", None, None))
    return jax.shard_map(
        on_device, mesh=mesh, in_specs=in_specs, out_specs=out_specs, check_vma=False
    )
```

profile of v0, /device:TPU:1, one launch (start us, length us, event | category | flops | bytes accessed | tf_op | source)
XLA Modules:
  0.0 602.6 jit_solution(1608577410166236295)
XLA Ops:
  34.6 9.3 %scatter_fusion = f32[1024,256]{1,0:T(8,128)S(1)} fusion(f32[1024,256]{1,0:T(8,128)S(1)} %bitcast.238, s32[1152]{0:T(1024)S(1)} %fusion.53, f32[1152,256]{1,0:T(8,128)S(1)} %constant_dynamic-update-slice_fusion), kind=kCustom, calls=%fused_computation.9 | custom fusion | flops 294912 | bytes 3543552 | tf_op jit(solution)/shard_map/scatter-add | solution.py:56
  50.2 69.9 %all-reduce.21.cloned.1.call-done = f32[256,256]{0,1:T(8,128)} async-done(((f32[256,256]{0,1:T(8,128)}), f32[256,256]{0,1:T(8,128)}) %all-reduce.21.cloned.1.call-update) | async-done | bytes 262160 | tf_op jit(solution)/shard_map/psum | solution.py:68
  134.8 6.9 %collective-permute-start.6 = (f32[160,256]{1,0:T(8,128)S(1)}, f32[160,256]{1,0:T(8,128)S(1)}, u32[]{:S(2)}, u32[]{:S(2)}) collective-permute-start(f32[160,256]{1,0:T(8,128)S(1)} %pad_maximum_fusion.6), channel_id=1, source_target_pairs={{0,8},{8,16},{16,24},{1,9},{9,17},{17,25},{2,10},{10,18},{18,26},{... | collective-permute-start | bytes 491528 | tf_op jit(solution)/shard_map/ppermute | solution.py:16
  148.5 9.7 %scatter_fusion.1 = f32[1024,256]{1,0:T(8,128)S(1)} fusion(f32[1024,256]{1,0:T(8,128)S(1)} %copy.27, s32[1152]{0:T(1024)S(1)} %fusion.53, f32[1152,256]{1,0:T(8,128)S(1)} %constant_dynamic-update-slice_fusion.9), kind=kCustom, calls=%fused_computation.10 | custom fusion | flops 294912 | bytes 3543552 | tf_op jit(solution)/shard_map/scatter-add | solution.py:56
  158.3 10.0 %fusion.12 = f32[1024,256]{0,1:T(8,128)} fusion(f32[1024,256]{1,0:T(8,128)S(1)} %scatter_fusion.1, f32[1,1,1024,1024]{3,2,1,0:T(8,128)} %param.9), kind=kOutput, calls=%fused_computation.30 | convolution fusion | flops 3221225472 | bytes 6291456 | tf_op jit(solution)/shard_map/dot_general | solution.py:96
  197.7 9.8 %scatter_fusion.2 = f32[1024,256]{1,0:T(8,128)S(1)} fusion(f32[1024,256]{1,0:T(8,128)S(1)} %copy.29, s32[1152]{0:T(1024)S(1)} %fusion.53, f32[1152,256]{1,0:T(8,128)} %constant_dynamic-update-slice_fusion.18), kind=kCustom, calls=%fused_computation.11 | custom fusion | flops 294912 | bytes 3543552 | tf_op jit(solution)/shard_map/scatter-add | solution.py:56
  208.7 9.1 %fusion.27 = f32[1024,256]{0,1:T(8,128)S(1)} fusion(f32[1,1,1024,1024]{3,2,1,0:T(8,128)} %param.10, f32[1024,256]{1,0:T(8,128)S(1)} %sub.12, f32[1024]{0:T(1024)S(1)} %bitcast.252), kind=kOutput, calls=%fused_computation.35 | convolution fusion | flops 3221749760 | bytes 6295552 | tf_op jit(solution)/shard_map/dot_general | solution.py:96
  243.9 9.5 %scatter_fusion.3 = f32[1024,256]{1,0:T(8,128)S(1)} fusion(f32[1024,256]{1,0:T(8,128)S(1)} %copy.31, s32[1152]{0:T(1024)S(1)} %fusion.53, f32[1152,256]{1,0:T(8,128)S(1)} %constant_dynamic-update-slice_fusion.27), kind=kCustom, calls=%fused_computation.12 | custom fusion | flops 294912 | bytes 3543552 | tf_op jit(solution)/shard_map/scatter-add | solution.py:56
  253.4 10.0 %fusion.15 = f32[1024,256]{0,1:T(8,128)} fusion(f32[1024,256]{1,0:T(8,128)S(1)} %scatter_fusion.3, f32[1,1,1024,1024]{3,2,1,0:T(8,128)} %param.9), kind=kOutput, calls=%fused_computation.31 | convolution fusion | flops 3221225472 | bytes 6291456 | tf_op jit(solution)/shard_map/dot_general | solution.py:96
  292.0 10.1 %scatter_fusion.4 = f32[1024,256]{1,0:T(8,128)S(1)} fusion(f32[1024,256]{1,0:T(8,128)S(1)} %copy.33, s32[1152]{0:T(1024)S(1)} %fusion.53, f32[1152,256]{1,0:T(8,128)} %constant_dynamic-update-slice_fusion.36), kind=kCustom, calls=%fused_computation.13 | custom fusion | flops 294912 | bytes 3543552 | tf_op jit(solution)/shard_map/scatter-add | solution.py:56
  305.3 5.9 all_gather.7
  312.3 67.5 %all-reduce.23.cloned.1.call-done = f32[256,256]{0,1:T(8,128)} async-done(((f32[256,256]{0,1:T(8,128)}), f32[256,256]{0,1:T(8,128)}) %all-reduce.23.cloned.1.call-update) | async-done | bytes 262160 | tf_op jit(solution)/shard_map/psum | solution.py:68
  398.4 6.9 %collective-permute-start.22 = (f32[160,256]{1,0:T(8,128)S(1)}, f32[160,256]{1,0:T(8,128)S(1)}, u32[]{:S(2)}, u32[]{:S(2)}) collective-permute-start(f32[160,256]{1,0:T(8,128)S(1)} %pad_maximum_fusion.22), channel_id=1, source_target_pairs={{0,8},{8,16},{16,24},{1,9},{9,17},{17,25},{2,10},{10,18},{18,26},{... | collective-permute-start | bytes 491528 | tf_op jit(solution)/shard_map/ppermute | solution.py:16
  414.0 9.8 %scatter_fusion.5 = f32[1024,256]{1,0:T(8,128)S(1)} fusion(f32[1024,256]{1,0:T(8,128)S(1)} %copy.35, s32[1152]{0:T(1024)S(1)} %fusion.53, f32[1152,256]{1,0:T(8,128)} %constant_dynamic-update-slice_fusion.45), kind=kCustom, calls=%fused_computation.14 | custom fusion | flops 294912 | bytes 3543552 | tf_op jit(solution)/shard_map/scatter-add | solution.py:56
  423.9 10.0 %fusion.18 = f32[1024,256]{0,1:T(8,128)} fusion(f32[1024,256]{1,0:T(8,128)S(1)} %scatter_fusion.5, f32[1,1,1024,1024]{3,2,1,0:T(8,128)} %param.9), kind=kOutput, calls=%fused_computation.32 | convolution fusion | flops 3221225472 | bytes 6291456 | tf_op jit(solution)/shard_map/dot_general | solution.py:96
  436.4 5.3 gather_fusion.6
  453.6 5.4 collective-permute-start.26
  467.7 11.6 %scatter_fusion.6 = f32[1024,256]{1,0:T(8,128)} fusion(f32[1024,256]{1,0:T(8,128)} %copy.37, s32[1152]{0:T(1024)S(1)} %fusion.53, f32[1152,256]{1,0:T(8,128)} %constant_dynamic-update-slice_fusion.54), kind=kCustom, calls=%fused_computation.15 | custom fusion | flops 294912 | bytes 3543552 | tf_op jit(solution)/shard_map/scatter-add | solution.py:56
  482.0 10.2 %fusion.33 = f32[1024,256]{0,1:T(8,128)} fusion(f32[1,1,1024,1024]{3,2,1,0:T(8,128)} %param.10, f32[1024,256]{1,0:T(8,128)S(1)} %sub.14, f32[1024]{0:T(1024)S(1)} %bitcast.255), kind=kOutput, calls=%fused_computation.37 | convolution fusion | flops 3221749760 | bytes 6295552 | tf_op jit(solution)/shard_map/dot_general | solution.py:96
  511.1 5.4 collective-permute-start.30
  525.2 11.6 %scatter_fusion.7 = f32[1024,256]{1,0:T(8,128)} fusion(f32[1024,256]{1,0:T(8,128)} %copy.39, s32[1152]{0:T(1024)S(1)} %fusion.53, f32[1152,256]{1,0:T(8,128)} %constant_dynamic-update-slice_fusion.63), kind=kCustom, calls=%fused_computation.16 | custom fusion | flops 294912 | bytes 3543552 | tf_op jit(solution)/shard_map/scatter-add | solution.py:56
  536.9 10.3 %fusion.21 = f32[1024,256]{0,1:T(8,128)} fusion(f32[1024,256]{1,0:T(8,128)} %scatter_fusion.7, f32[1,1,1024,1024]{3,2,1,0:T(8,128)} %param.9), kind=kOutput, calls=%fused_computation.33 | convolution fusion | flops 3221225472 | bytes 6291456 | tf_op jit(solution)/shard_map/dot_general | solution.py:96
  566.2 5.4 collective-permute-start.34
  580.3 11.4 %scatter_fusion.8 = f32[1024,256]{1,0:T(8,128)} fusion(f32[1024,256]{1,0:T(8,128)} %copy.41, s32[1152]{0:T(1024)S(1)} %fusion.53, f32[1152,256]{1,0:T(8,128)} %constant_dynamic-update-slice_fusion.72), kind=kCustom, calls=%fused_computation.17 | custom fusion | flops 294912 | bytes 3543552 | tf_op jit(solution)/shard_map/scatter-add | solution.py:56
  (332 shorter events, 255.8 us)
Async XLA Ops:
  7.2 112.9 %all-reduce.21.cloned.1.call-start = ((), (), s32[]{:S(2)}) async-start(), calls=%async_computation | async-start | bytes 524288 | tf_op jit(solution)/shard_map/psum | solution.py:68
  12.3 6.8 %collective-permute-start = (f32[160,256]{1,0:T(8,128)S(1)}, f32[160,256]{1,0:T(8,128)S(1)}, u32[]{:S(2)}, u32[]{:S(2)}) collective-permute-start(f32[160,256]{1,0:T(8,128)S(1)} %pad_maximum_fusion), channel_id=1, source_target_pairs={{0,1},{1,2},{2,3},{3,4},{4,5},{5,6},{6,7},{8,9},{9,10},{10,11},{11... | collective-permute-start | bytes 491528 | tf_op jit(solution)/shard_map/ppermute | solution.py:16
  16.3 6.6 %collective-permute-start.1 = (f32[160,256]{1,0:T(8,128)S(1)}, f32[160,256]{1,0:T(8,128)S(1)}, u32[]{:S(2)}, u32[]{:S(2)}) collective-permute-start(f32[160,256]{1,0:T(8,128)S(1)} %pad_maximum_fusion.1), channel_id=1, source_target_pairs={{1,0},{2,1},{3,2},{4,3},{5,4},{6,5},{7,6},{9,8},{10,9},{11,10},{12... | collective-permute-start | bytes 491528 | tf_op jit(solution)/shard_map/ppermute | solution.py:16
  22.9 7.1 %collective-permute-start.2 = (f32[160,256]{1,0:T(8,128)S(1)}, f32[160,256]{1,0:T(8,128)S(1)}, u32[]{:S(2)}, u32[]{:S(2)}) collective-permute-start(f32[160,256]{1,0:T(8,128)S(1)} %pad_maximum_fusion.2), channel_id=1, source_target_pairs={{0,8},{8,16},{16,24},{1,9},{9,17},{17,25},{2,10},{10,18},{18,26},{... | collective-permute-start | bytes 491528 | tf_op jit(solution)/shard_map/ppermute | solution.py:16
  27.9 6.6 %collective-permute-start.3 = (f32[160,256]{1,0:T(8,128)S(1)}, f32[160,256]{1,0:T(8,128)S(1)}, u32[]{:S(2)}, u32[]{:S(2)}) collective-permute-start(f32[160,256]{1,0:T(8,128)S(1)} %pad_maximum_fusion.3), channel_id=1, source_target_pairs={{8,0},{16,8},{24,16},{9,1},{17,9},{25,17},{10,2},{18,10},{26,18},{... | collective-permute-start | bytes 491528 | tf_op jit(solution)/shard_map/ppermute | solution.py:16
  50.2 329.6 %all-reduce.23.cloned.1.call-start = ((), (), s32[]{:S(2)}) async-start(), calls=%async_computation.1 | async-start | bytes 524288 | tf_op jit(solution)/shard_map/psum | solution.py:68
  134.8 9.2 %collective-permute-start.6 = (f32[160,256]{1,0:T(8,128)S(1)}, f32[160,256]{1,0:T(8,128)S(1)}, u32[]{:S(2)}, u32[]{:S(2)}) collective-permute-start(f32[160,256]{1,0:T(8,128)S(1)} %pad_maximum_fusion.6), channel_id=1, source_target_pairs={{0,8},{8,16},{16,24},{1,9},{9,17},{17,25},{2,10},{10,18},{18,26},{... | collective-permute-start | bytes 491528 | tf_op jit(solution)/shard_map/ppermute | solution.py:16
  141.7 6.6 %collective-permute-start.7 = (f32[160,256]{1,0:T(8,128)S(1)}, f32[160,256]{1,0:T(8,128)S(1)}, u32[]{:S(2)}, u32[]{:S(2)}) collective-permute-start(f32[160,256]{1,0:T(8,128)S(1)} %pad_maximum_fusion.7), channel_id=1, source_target_pairs={{8,0},{16,8},{24,16},{9,1},{17,9},{25,17},{10,2},{18,10},{26,18},{... | collective-permute-start | bytes 491528 | tf_op jit(solution)/shard_map/ppermute | solution.py:16
  175.5 8.2 %collective-permute-start.8 = (f32[160,256]{1,0:T(8,128)S(1)}, f32[160,256]{1,0:T(8,128)S(1)}, u32[]{:S(2)}, u32[]{:S(2)}) collective-permute-start(f32[160,256]{1,0:T(8,128)S(1)} %pad_maximum_fusion.8), channel_id=1, source_target_pairs={{0,1},{1,2},{2,3},{3,4},{4,5},{5,6},{6,7},{8,9},{9,10},{10,11},{11... | collective-permute-start | bytes 491528 | tf_op jit(solution)/shard_map/ppermute | solution.py:16
  189.0 6.6 %collective-permute-start.11 = (f32[160,256]{1,0:T(8,128)S(1)}, f32[160,256]{1,0:T(8,128)S(1)}, u32[]{:S(2)}, u32[]{:S(2)}) collective-permute-start(f32[160,256]{1,0:T(8,128)S(1)} %pad_maximum_fusion.11), channel_id=1, source_target_pairs={{8,0},{16,8},{24,16},{9,1},{17,9},{25,17},{10,2},{18,10},{26,18},{... | collective-permute-start | bytes 491528 | tf_op jit(solution)/shard_map/ppermute | solution.py:16
  232.2 7.2 %collective-permute-start.14 = (f32[160,256]{1,0:T(8,128)S(1)}, f32[160,256]{1,0:T(8,128)S(1)}, u32[]{:S(2)}, u32[]{:S(2)}) collective-permute-start(f32[160,256]{1,0:T(8,128)S(1)} %pad_maximum_fusion.14), channel_id=1, source_target_pairs={{0,8},{8,16},{16,24},{1,9},{9,17},{17,25},{2,10},{10,18},{18,26},{... | collective-permute-start | bytes 491528 | tf_op jit(solution)/shard_map/ppermute | solution.py:16
  237.1 6.6 %collective-permute-start.15 = (f32[160,256]{1,0:T(8,128)S(1)}, f32[160,256]{1,0:T(8,128)S(1)}, u32[]{:S(2)}, u32[]{:S(2)}) collective-permute-start(f32[160,256]{1,0:T(8,128)S(1)} %pad_maximum_fusion.15), channel_id=1, source_target_pairs={{8,0},{16,8},{24,16},{9,1},{17,9},{25,17},{10,2},{18,10},{26,18},{... | collective-permute-start | bytes 491528 | tf_op jit(solution)/shard_map/ppermute | solution.py:16
  270.6 7.5 %collective-permute-start.16 = (f32[160,256]{1,0:T(8,128)S(1)}, f32[160,256]{1,0:T(8,128)S(1)}, u32[]{:S(2)}, u32[]{:S(2)}) collective-permute-start(f32[160,256]{1,0:T(8,128)S(1)} %pad_maximum_fusion.16), channel_id=1, source_target_pairs={{0,1},{1,2},{2,3},{3,4},{4,5},{5,6},{6,7},{8,9},{9,10},{10,11},{11... | collective-permute-start | bytes 491528 | tf_op jit(solution)/shard_map/ppermute | solution.py:16
  398.4 9.2 %collective-permute-start.22 = (f32[160,256]{1,0:T(8,128)S(1)}, f32[160,256]{1,0:T(8,128)S(1)}, u32[]{:S(2)}, u32[]{:S(2)}) collective-permute-start(f32[160,256]{1,0:T(8,128)S(1)} %pad_maximum_fusion.22), channel_id=1, source_target_pairs={{0,8},{8,16},{16,24},{1,9},{9,17},{17,25},{2,10},{10,18},{18,26},{... | collective-permute-start | bytes 491528 | tf_op jit(solution)/shard_map/ppermute | solution.py:16
  405.3 6.6 %collective-permute-start.23 = (f32[160,256]{1,0:T(8,128)S(1)}, f32[160,256]{1,0:T(8,128)S(1)}, u32[]{:S(2)}, u32[]{:S(2)}) collective-permute-start(f32[160,256]{1,0:T(8,128)S(1)} %pad_maximum_fusion.23), channel_id=1, source_target_pairs={{8,0},{16,8},{24,16},{9,1},{17,9},{25,17},{10,2},{18,10},{26,18},{... | collective-permute-start | bytes 491528 | tf_op jit(solution)/shard_map/ppermute | solution.py:16
  443.2 8.2 %collective-permute-start.24 = (f32[160,256]{1,0:T(8,128)S(1)}, f32[160,256]{1,0:T(8,128)S(1)}, u32[]{:S(2)}, u32[]{:S(2)}) collective-permute-start(f32[160,256]{1,0:T(8,128)S(1)} %pad_maximum_fusion.24), channel_id=1, source_target_pairs={{0,1},{1,2},{2,3},{3,4},{4,5},{5,6},{6,7},{8,9},{9,10},{10,11},{11... | collective-permute-start | bytes 491528 | tf_op jit(solution)/shard_map/ppermute | solution.py:16
  453.6 7.7 %collective-permute-start.26 = (f32[160,256]{1,0:T(8,128)S(1)}, f32[160,256]{1,0:T(8,128)S(1)}, u32[]{:S(2)}, u32[]{:S(2)}) collective-permute-start(f32[160,256]{1,0:T(8,128)S(1)} %pad_maximum_fusion.26), channel_id=1, source_target_pairs={{0,8},{8,16},{16,24},{1,9},{9,17},{17,25},{2,10},{10,18},{18,26},{... | collective-permute-start | bytes 491528 | tf_op jit(solution)/shard_map/ppermute | solution.py:16
  459.0 6.6 %collective-permute-start.27 = (f32[160,256]{1,0:T(8,128)S(1)}, f32[160,256]{1,0:T(8,128)S(1)}, u32[]{:S(2)}, u32[]{:S(2)}) collective-permute-start(f32[160,256]{1,0:T(8,128)S(1)} %pad_maximum_fusion.27), channel_id=1, source_target_pairs={{8,0},{16,8},{24,16},{9,1},{17,9},{25,17},{10,2},{18,10},{26,18},{... | collective-permute-start | bytes 491528 | tf_op jit(solution)/shard_map/ppermute | solution.py:16
  501.6 7.4 %collective-permute-start.28 = (f32[160,256]{1,0:T(8,128)S(1)}, f32[160,256]{1,0:T(8,128)S(1)}, u32[]{:S(2)}, u32[]{:S(2)}) collective-permute-start(f32[160,256]{1,0:T(8,128)S(1)} %pad_maximum_fusion.28), channel_id=1, source_target_pairs={{0,1},{1,2},{2,3},{3,4},{4,5},{5,6},{6,7},{8,9},{9,10},{10,11},{11... | collective-permute-start | bytes 491528 | tf_op jit(solution)/shard_map/ppermute | solution.py:16
  511.1 7.7 %collective-permute-start.30 = (f32[160,256]{1,0:T(8,128)S(1)}, f32[160,256]{1,0:T(8,128)S(1)}, u32[]{:S(2)}, u32[]{:S(2)}) collective-permute-start(f32[160,256]{1,0:T(8,128)S(1)} %pad_maximum_fusion.30), channel_id=1, source_target_pairs={{0,8},{8,16},{16,24},{1,9},{9,17},{17,25},{2,10},{10,18},{18,26},{... | collective-permute-start | bytes 491528 | tf_op jit(solution)/shard_map/ppermute | solution.py:16
  516.6 6.6 %collective-permute-start.31 = (f32[160,256]{1,0:T(8,128)S(1)}, f32[160,256]{1,0:T(8,128)S(1)}, u32[]{:S(2)}, u32[]{:S(2)}) collective-permute-start(f32[160,256]{1,0:T(8,128)S(1)} %pad_maximum_fusion.31), channel_id=1, source_target_pairs={{8,0},{16,8},{24,16},{9,1},{17,9},{25,17},{10,2},{18,10},{26,18},{... | collective-permute-start | bytes 491528 | tf_op jit(solution)/shard_map/ppermute | solution.py:16
  556.6 7.5 %collective-permute-start.32 = (f32[160,256]{1,0:T(8,128)S(1)}, f32[160,256]{1,0:T(8,128)S(1)}, u32[]{:S(2)}, u32[]{:S(2)}) collective-permute-start(f32[160,256]{1,0:T(8,128)S(1)} %pad_maximum_fusion.32), channel_id=1, source_target_pairs={{0,1},{1,2},{2,3},{3,4},{4,5},{5,6},{6,7},{8,9},{9,10},{10,11},{11... | collective-permute-start | bytes 491528 | tf_op jit(solution)/shard_map/ppermute | solution.py:16
  566.2 7.7 %collective-permute-start.34 = (f32[160,256]{1,0:T(8,128)S(1)}, f32[160,256]{1,0:T(8,128)S(1)}, u32[]{:S(2)}, u32[]{:S(2)}) collective-permute-start(f32[160,256]{1,0:T(8,128)S(1)} %pad_maximum_fusion.34), channel_id=1, source_target_pairs={{0,8},{8,16},{16,24},{1,9},{9,17},{17,25},{2,10},{10,18},{18,26},{... | collective-permute-start | bytes 491528 | tf_op jit(solution)/shard_map/ppermute | solution.py:16
  571.6 6.6 %collective-permute-start.35 = (f32[160,256]{1,0:T(8,128)S(1)}, f32[160,256]{1,0:T(8,128)S(1)}, u32[]{:S(2)}, u32[]{:S(2)}) collective-permute-start(f32[160,256]{1,0:T(8,128)S(1)} %pad_maximum_fusion.35), channel_id=1, source_target_pairs={{8,0},{16,8},{24,16},{9,1},{17,9},{25,17},{10,2},{18,10},{26,18},{... | collective-permute-start | bytes 491528 | tf_op jit(solution)/shard_map/ppermute | solution.py:16
  (37 other events, 356.3 us)
Sparse Core Ops, SparseCore 0:
  50.3 69.7 all-reduce.20
  312.4 67.3 all-reduce.22
where the time goes:
time: 613 us; the launch traced here: 603 us
  waiting for transfers between devices  199 us (32%)
  other arithmetic  119 us (19%)
  starting transfers between devices  106 us (17%)
  local copies, waits for them, and re-layouts  84.4 us (14%)
  matrix products  68.1 us (11%)
  between operations  15.9 us (3%)
  blocking collectives  10.1 us (2%)
    psum x2, waiting for transfers between devices, coarse_solve(): summed = lax.psum(partial_sol, 'col')  137 us
    ppermute x36, starting transfers between devices, passed_along(): lax.ppermute(value, axis, [(source, source + steps) for source in range(l...  106 us
    scatter-add x9, other arithmetic, neighbour_sum(): return values.at[rows_local.reshape(-1)].add(stacked)  92.9 us
    ppermute x36, waiting for transfers between devices, passed_along(): lax.ppermute(value, axis, [(source, source + steps) for source in range(l...  61.5 us
    dot_general x8, matrix products, apply_matrix(): jnp.dot(matrix, values, precision=PRECISE, preferred_element_type=jnp.flo...  61 us
    gather x9, local copies, waits for them, and re-layouts, neighbour_sum(): packets = values[rows_local] * live_mask[..., None]  38.7 us
    unnamed x102, local copies, waits for them, and re-layouts  28.2 us
  transfers between devices with their start and end apart: 38, of which 38 were waited for; matrix products, arithmetic and copies ran while one was open for 4% of the time, Pallas kernels for 0%

commit v1 on v0

v1 whole, which is shorter than its diff:
```python
import functools

import jax
import jax.numpy as jnp
from jax import lax
from jax.experimental import pallas as pl
from jax.experimental.pallas import tpu as pltpu
from jax.sharding import PartitionSpec as P

CORNER = 16
STEPS = 2
F32 = jnp.float32
BF16 = jnp.bfloat16
MESH = pl.DeviceIdType.MESH

DIRS = ((-1, 0), (0, -1), (0, 1), (1, 0), (-1, -1), (-1, 1), (1, -1), (1, 1))
OPPOSITE = (3, 2, 1, 0, 7, 6, 5, 4)
LANES = 128


def split(value):
    high = value.astype(BF16)
    low = (value - high.astype(F32)).astype(BF16)
    return high, low


def dot(left, right):
    return jnp.dot(left, right, preferred_element_type=F32)


def dot3(left, right):
    (lh, ll), (rh, rl) = left, right
    return dot(lh, rh) + (dot(lh, rl) + dot(ll, rh))


def pick(onehot, value):
    high, low = value
    return dot(onehot, high) + dot(onehot, low)


def kernel(
    rows, cols, n, r, k, share,
    load_ref, schur_hbm, solver_hbm, modes_ref, tile_ref, slots_ref, weight_ref,
    iter_ref, res_ref,
    mat_s, mat_m, s_hi, s_lo, m_hi, m_lo, gather_ref, scatter_ref,
    wide_ref, ext_hi, ext_lo, ext_t_hi, ext_t_lo, cor_hi, cor_lo, cor_t_hi, cor_t_lo,
    tile_t_hi, tile_t_lo, local_ref,
    mode_send, mode_recv, a_send, a_recv, x_send, x_recv, gat, part, red,
    local_sem, mode_ss, mode_rs, a_ss, a_rs, x_ss, x_rs, g_ss, g_rs, p_ss, p_rs,
):
    a = lax.axis_index("row")
    b = lax.axis_index("col")
    copy_s = pltpu.make_async_copy(schur_hbm, mat_s, local_sem.at[0])
    copy_m = pltpu.make_async_copy(solver_hbm, mat_m, local_sem.at[1])
    copy_s.start()
    copy_m.start()

    def exists(d):
        p, q = a + DIRS[d][0], b + DIRS[d][1]
        return (p >= 0) & (p < rows) & (q >= 0) & (q < cols)

    def there(d):
        return (a + DIRS[d][0], b + DIRS[d][1])

    mode_recv[...] = jnp.zeros_like(mode_recv)
    a_recv[...] = jnp.zeros_like(a_recv)
    x_recv[...] = jnp.zeros_like(x_recv)

    barrier = pltpu.get_barrier_semaphore()
    for off in range(1, rows):
        pl.semaphore_signal(
            barrier, inc=1, device_id=(lax.rem(a + off, rows), b), device_id_type=MESH
        )
    for off in range(1, cols):
        pl.semaphore_signal(
            barrier, inc=1, device_id=(a, lax.rem(b + off, cols)), device_id_type=MESH
        )
    for d in range(4, 8):
        @pl.when(exists(d))
        def _():
            pl.semaphore_signal(barrier, inc=1, device_id=there(d), device_id_type=MESH)

    slot_pad = slots_ref.shape[1]
    slots = slots_ref[...]
    scatter_ref[...] = jnp.where(
        lax.broadcasted_iota(jnp.int32, (n, slot_pad), 0).astype(F32) == slots, 1.0, 0.0
    ).astype(BF16)
    slots_t = jnp.broadcast_to(slots, (LANES, slot_pad)).T
    for i in range(n // LANES):
        ids = (lax.broadcasted_iota(jnp.int32, (slot_pad, LANES), 1) + i * LANES).astype(F32)
        gather_ref[:, i * LANES:(i + 1) * LANES] = jnp.where(ids == slots_t, 1.0, 0.0).astype(BF16)
    weight = weight_ref[...]
    weight_t = jnp.broadcast_to(weight, (LANES, n)).T
    for i in range(r // LANES):
        wide_ref[:, i * LANES:(i + 1) * LANES] = weight_t
    zw = modes_ref[...] * weight
    zw2 = split(zw)
    at_slots = pick_right(zw2, scatter_ref)
    for d in range(4):
        mode_send[d] = at_slots[:, d * share:(d + 1) * share]

    diagonals = sum(exists(d).astype(jnp.int32) for d in range(4, 8))
    pl.semaphore_wait(barrier, rows + cols - 2 + diagonals)

    def mode_copy(d, out):
        e = OPPOSITE[d]
        return pltpu.make_async_remote_copy(
            src_ref=mode_send.at[d],
            dst_ref=mode_recv.at[e if out else d],
            send_sem=mode_ss.at[d],
            recv_sem=mode_rs.at[e if out else d],
            device_id=there(d),
            device_id_type=MESH,
        )

    def for_dirs(count, body):
        for d in range(count):
            @pl.when(exists(d))
            def _():
                body(d)

    for_dirs(4, lambda d: mode_copy(d, True).start())

    def exchange(send, recv, ss, rs, wide):
        def span(d):
            if d < 4:
                return pl.ds(d * wide, wide)
            return pl.ds(4 * wide + (d - 4) * CORNER, CORNER)

        def copy(d, out):
            e = OPPOSITE[d] if out else d
            return pltpu.make_async_remote_copy(
                src_ref=send.at[span(d)],
                dst_ref=recv.at[span(e)],
                send_sem=ss.at[d],
                recv_sem=rs.at[e],
                device_id=there(d),
                device_id_type=MESH,
            )

        def start():
            for_dirs(8, lambda d: copy(d, True).start())

        def wait():
            for_dirs(8, lambda d: copy(d, False).wait_recv())
            for_dirs(8, lambda d: copy(d, True).wait_send())

        return start, wait

    slot_count = 4 * share + 4 * CORNER
    corner_g = gather_ref[4 * share:slot_count, :]
    corner_m = pick(corner_g, split(zw.T))
    c_hi, c_lo = split(corner_m)
    cor_hi[...] = c_hi
    cor_lo[...] = c_lo
    t_hi, t_lo = split(corner_m.T)
    cor_t_hi[...] = t_hi
    cor_t_lo[...] = t_lo
    t_hi, t_lo = split(tile_ref[...].T)
    tile_t_hi[...] = t_hi
    tile_t_lo[...] = t_lo
    local_ref[...] = -load_ref[...]
    iter_ref[...] = jnp.zeros_like(iter_ref)
    res_ref[...] = jnp.zeros_like(res_ref)

    copy_s.wait()
    hi, lo = split(mat_s[...])
    s_hi[...] = hi
    s_lo[...] = lo
    for_dirs(4, lambda d: mode_copy(d, False).wait_recv())
    for_dirs(4, lambda d: mode_copy(d, True).wait_send())

    ext_hi[0:k, :] = zw2[0]
    ext_lo[0:k, :] = zw2[1]
    for d in range(4):
        m_h, m_l = split(mode_recv[d])
        onehot = gather_ref[d * share:(d + 1) * share, :]
        ext_hi[(d + 1) * k:(d + 2) * k, :] = dot(m_h, onehot).astype(BF16)
        ext_lo[(d + 1) * k:(d + 2) * k, :] = dot(m_l, onehot).astype(BF16)
    ext_hi[5 * k:, :] = corner_g
    ext_lo[5 * k:, :] = jnp.zeros_like(corner_g)
    ext_t_hi[...] = ext_hi[...].astype(F32).T.astype(BF16)
    ext_t_lo[...] = ext_lo[...].astype(F32).T.astype(BF16)

    copy_m.wait()
    hi, lo = split(mat_m[...])
    m_hi[...] = hi
    m_lo[...] = lo

    def assemble(value, index):
        send, recv = a_send.at[index], a_recv.at[index]
        start, wait = exchange(send, recv, a_ss.at[index], a_rs.at[index], share)
        send[...] = pick(gather_ref[0:slot_count, :], split(value))
        start()

        def finish():
            wait()
            return value + pick(scatter_ref[...], split(recv[...]))

        return finish

    def step(t, carry):
        gat_t, part_t, red_t = gat.at[t], part.at[t], red.at[t]
        first = split(local_ref[...])
        out = dot3((ext_hi[...], ext_lo[...]), first)
        send, recv = x_send.at[2 * t], x_recv.at[2 * t]
        start, wait = exchange(send, recv, x_ss.at[2 * t], x_rs.at[2 * t], k)
        send[...] = out[k:, :]
        start()
        own = dot3((ext_hi[0:k, :], ext_lo[0:k, :]), split(res_ref[...])) - out[0:k, :]
        wait()
        near = recv[0:k, :]
        for d in range(1, 4):
            near = near + recv[d * k:(d + 1) * k, :]
        near = near + dot3((cor_t_hi[...], cor_t_lo[...]), split(recv[4 * k:, :]))
        gat_t[a] = own - near

        def gather_copy(off, out):
            peer = lax.rem(a + off, rows) if out else lax.rem(a + rows - off, rows)
            return pltpu.make_async_remote_copy(
                src_ref=gat_t.at[a],
                dst_ref=gat_t.at[a if out else peer],
                send_sem=g_ss.at[t, off],
                recv_sem=g_rs.at[t, off],
                device_id=(peer, b),
                device_id_type=MESH,
            )

        for off in range(1, rows):
            gather_copy(off, True).start()
        for off in range(1, rows):
            gather_copy(off, False).wait_recv()
        for off in range(1, rows):
            gather_copy(off, True).wait_send()
        rhs = split(gat_t[...].reshape(rows * k, r))
        part_t[...] = dot3((tile_t_hi[...], tile_t_lo[...]), rhs).reshape(cols, k, r)

        def part_copy(off, out):
            peer = lax.rem(b + off, cols) if out else lax.rem(b + cols - off, cols)
            return pltpu.make_async_remote_copy(
                src_ref=part_t.at[peer],
                dst_ref=red_t.at[off],
                send_sem=p_ss.at[t, off],
                recv_sem=p_rs.at[t, off],
                device_id=(a, peer),
                device_id_type=MESH,
            )

        for off in range(1, cols):
            part_copy(off, True).start()
        sol = part_t[b]
        for off in range(1, cols):
            part_copy(off, False).wait_recv()
            sol = sol + red_t[off]
        for off in range(1, cols):
            part_copy(off, True).wait_send()

        send, recv = x_send.at[2 * t + 1], x_recv.at[2 * t + 1]
        start, wait = exchange(send, recv, x_ss.at[2 * t + 1], x_rs.at[2 * t + 1], k)
        for d in range(4):
            send[d * k:(d + 1) * k, :] = sol
        sol2 = split(sol)
        send[4 * k:, :] = dot3((cor_hi[...], cor_lo[...]), sol2)
        start()
        wait()
        all_sol = split(jnp.concatenate([sol, recv[...]], axis=0))
        corr = dot3((ext_t_hi[...], ext_t_lo[...]), all_sol)
        iter_ref[...] += corr
        moved = local_ref[...] + dot3((s_hi[...], s_lo[...]), split(corr))
        res_ref[...] -= assemble(moved, 2 * t)()
        weighted = split(wide_ref[...] * res_ref[...])
        update = assemble(
            wide_ref[...] * dot3((m_hi[...], m_lo[...]), weighted), 2 * t + 1
        )()
        iter_ref[...] += update
        local_ref[...] = dot3((s_hi[...], s_lo[...]), split(update))
        return carry

    lax.fori_loop(0, STEPS, step, 0)
    res_ref[...] -= assemble(local_ref[...], 2 * STEPS)()


def pick_right(value, onehot_ref):
    return dot(value[0], onehot_ref[...]) + dot(value[1], onehot_ref[...])


def on_device(
    rows, cols,
    local_load,
    schur_operator,
    local_solver,
    coarse_modes,
    coarse_inverse,
    share_rows,
    share_count,
    multiplicity,
):
    n, r = local_load.shape[2:]
    k = coarse_modes.shape[2]
    share = share_rows.shape[-1]
    live = lax.broadcasted_iota(jnp.int32, share_rows.shape[2:], 2) < share_count[0, 0][..., None]
    listed = jnp.where(live, share_rows[0, 0], -1).astype(F32)
    pieces = [
        listed[p + 1, q + 1, : share if d < 4 else CORNER] for d, (p, q) in enumerate(DIRS)
    ]
    slot_count = 4 * share + 4 * CORNER
    slot_pad = -(-slot_count // LANES) * LANES
    slots = jnp.pad(jnp.concatenate(pieces), (0, slot_pad - slot_count), constant_values=-1.0)
    weight = 1.0 / multiplicity[0, 0].astype(F32)
    width = 5 * k + 4 * CORNER
    vm = pltpu.VMEM
    dma = pltpu.SemaphoreType.DMA
    scratch = [
        vm((n, n), F32), vm((n, n), F32),
        vm((n, n), BF16), vm((n, n), BF16), vm((n, n), BF16), vm((n, n), BF16),
        vm((slot_pad, n), BF16), vm((n, slot_pad), BF16),
        vm((n, r), F32),
        vm((width, n), BF16), vm((width, n), BF16), vm((n, width), BF16), vm((n, width), BF16),
        vm((4 * CORNER, k), BF16), vm((4 * CORNER, k), BF16),
        vm((k, 4 * CORNER), BF16), vm((k, 4 * CORNER), BF16),
        vm((cols * k, rows * k), BF16), vm((cols * k, rows * k), BF16),
        vm((n, r), F32),
        vm((4, k, share), F32), vm((4, k, share), F32),
        vm((2 * STEPS + 1, slot_count, r), F32), vm((2 * STEPS + 1, slot_pad, r), F32),
        vm((2 * STEPS, width - k, r), F32), vm((2 * STEPS, width - k, r), F32),
        vm((STEPS, rows, k, r), F32),
        vm((STEPS, cols, k, r), F32), vm((STEPS, cols, k, r), F32),
        dma((2,)), dma((4,)), dma((4,)),
        dma((2 * STEPS + 1, 8)), dma((2 * STEPS + 1, 8)),
        dma((2 * STEPS, 8)), dma((2 * STEPS, 8)),
        dma((STEPS, rows)), dma((STEPS, rows)),
        dma((STEPS, cols)), dma((STEPS, cols)),
    ]
    in_vmem = pl.BlockSpec(memory_space=pltpu.VMEM)
    in_place = pl.BlockSpec(memory_space=pl.ANY)
    iterate, residual = pl.pallas_call(
        functools.partial(kernel, rows, cols, n, r, k, share),
        out_shape=[jax.ShapeDtypeStruct((n, r), F32)] * 2,
        in_specs=[in_vmem, in_place, in_place, in_vmem, in_vmem, in_vmem, in_vmem],
        out_specs=[in_vmem] * 2,
        scratch_shapes=scratch,
        compiler_params=pltpu.CompilerParams(
            collective_id=0, has_side_effects=True, vmem_limit_bytes=60 * 2**20
        ),
    )(
        local_load[0, 0],
        schur_operator[0, 0],
        local_solver[0, 0],
        coarse_modes[0, 0],
        coarse_inverse[0, 0].reshape(rows * k, cols * k),
        slots[None, :],
        weight[None, :],
    )
    return (iterate[None, None], residual[None, None])


def solution(mesh):
    rows, cols = mesh.shape["row"], mesh.shape["col"]
    in_specs = (
        P("row", "col", None, None),
        P("row", "col", None, None),
        P("row", "col", None, None),
        P("row", "col", None, None),
        P("row", "col", None, None, None),
        P("row", "col", None, None, None),
        P("row", "col", None, None),
        P("row", "col", None),
    )
    out_specs = (P("row", "col", None, None), P("row", "col", None, None))
    return jax.shard_map(
        functools.partial(on_device, rows, cols),
        mesh=mesh, in_specs=in_specs, out_specs=out_specs, check_vma=False,
    )
```

time: 613 us -> 138 us (0.23)
  the two profiles are of different devices: /device:TPU:1 before, /device:TPU:17 now
where the time goes in v1:
time: 138 us
  Pallas kernels  129 us (93%)
  local copies, waits for them, and re-layouts  5.89 us (4%)
  other arithmetic  2.05 us (1%)
    pallas_call x1, Pallas kernels, on_device(): pl.pallas_call(functools.partial(kernel, rows, cols, n, r, k, share), out...  129 us
    unnamed x3, local copies, waits for them, and re-layouts  5.21 us

profile of v1, /device:TPU:17, one launch (start us, length us, event | category | flops | bytes accessed | tf_op | source)
XLA Modules:
  0.0 137.6 jit_solution(12743524838097361679)
XLA Ops:
  0.6 0.7 copy.14
  1.3 0.8 fusion
  2.1 0.1 concatenate.3
  2.2 0.6 broadcast_in_dim.15.slots_ref
  2.8 1.3 divide_bitcast_fusion.weight_ref
  4.0 129.0 %shard_map.95 = (f32[1024,256]{1,0:T(8,128)}, f32[1024,256]{1,0:T(8,128)}) custom-call(f32[1024,256]{1,0:T(8,128)} %bitcast.34, f32[1024,1024]{1,0:T(8,128)} %bitcast.32, f32[1024,1024]{1,0:T(8,128)} %bitcast.33, f32[32,1024]{1,0:T(8,128)} %bitcast.37, f32[128,256]{1,0:T(8,128)} %bitcast.38, f32[1,640]{1,0:T(1,128)} %broadcast_in_dim.15.slots_ref, ...), custom_call_target="tpu_custom_call" | custom-call | tf_op jit(solution)/shard_map/pallas_call | solution.py:336
  133.1 2.3 %copy.17 = f32[1,1,1024,256]{3,2,1,0:T(8,128)} copy(f32[1,1,1024,256]{3,2,1,0:T(8,128)} %bitcast.36) | data formatting | bytes 2097152
  135.4 2.3 %copy.18 = f32[1,1,1024,256]{3,2,1,0:T(8,128)} copy(f32[1,1,1024,256]{3,2,1,0:T(8,128)} %bitcast.35) | data formatting | bytes 2097152
  (3 shorter events, 0.0 us)
